TPU v7x, 32 devices: a whole 2x2x4 slice. The times are simulated.
32 devices in a mesh: seq: 16 (over z, y, x), dp: 2 (over core).
Axes of the slice: x: 2, y: 2, z: 4, core: 2. Of those that a mesh axis runs over, the one named last changes fastest.
Arguments:
- queries: bfloat16 [2, 6144, 1024], P('dp', 'seq'), may hold values from -6 to 6
- keys: bfloat16 [2, 6144, 1024], P('dp', 'seq'), may hold values from -6 to 6
- values: bfloat16 [2, 6144, 1024], P('dp', 'seq'), may hold values from -6 to 6
- out_grad: bfloat16 [2, 6144, 1024], P('dp', 'seq'), may hold values from -6 to 6
- proj_weight: bfloat16 [1024, 1024], replicated, may hold values from -0.1875 to 0.1875
- lengths: int32 [2, 32], P('dp'), may hold values from 1 to 768, 6144 in all within a row
Outputs:
- query_grads: bfloat16 [2, 6144, 1024], P('dp', 'seq')
- key_grads: bfloat16 [2, 6144, 1024], P('dp', 'seq')
- value_grads: bfloat16 [2, 6144, 1024], P('dp', 'seq')
- weight_grad: float32 [1024, 1024], P(('seq', 'dp'))
Inputs may be any that keep to these rules, and one draw needn't show every extreme that they name: In each stream the 32 utterance lengths cover the 6144 frames end to end; the longest is exactly 768.
All inputs are finite; a program needn't handle non-finite values.
Results may differ from a plain program's by a relative error of at most 0.02.
Values may be sent and summed in bfloat16 or wider, within the bound.
A program may use at most 128 MiB of HBM per device.

v0:
```python
import jax
import jax.numpy as jnp
from jax import lax
from jax.sharding import PartitionSpec as P

HEADS = 8
WINDOW = 256


NEG_FILL = -1e30


def extended(shard, sides, width):
    for axis, dim in sides:
        peers, length = (lax.axis_size(axis), shard.shape[dim])
        up = [(i, (i + 1) % peers) for i in range(peers - 1)]
        down = [(j, i) for i, j in up]
        last = lax.slice_in_dim(shard, length - width, length, axis=dim)
        leading = lax.slice_in_dim(shard, 0, width, axis=dim)
        before = lax.ppermute(last, axis, up)
        after = lax.ppermute(leading, axis, down)
        shard = jnp.concatenate([before, shard, after], axis=dim)
    return shard


def from_behind(shard, axis, by):
    peers = lax.axis_size(axis)
    pairs = [(i, i + by) for i in range(peers) if 0 <= i + by < peers]
    return lax.ppermute(shard, axis, pairs)


def inner_last(left, right):
    return lax.dot_general(
        left, right, (((1,), (1,)), ((), ())), preferred_element_type=jnp.float32
    )


def inner_first(left, right):
    return lax.dot_general(
        left, right, (((0,), (0,)), ((), ())), preferred_element_type=jnp.float32
    )


def segment_of(utter_ends, spots):
    return jnp.sum((utter_ends[None, :] <= spots[:, None]).astype(jnp.int32), axis=1)


def visible(query_spots, key_spots, utter_ends, grid_total, window):
    query_seg = segment_of(utter_ends, query_spots)
    key_seg = segment_of(utter_ends, key_spots)
    inside_query = (query_spots >= 0) & (query_spots < grid_total)
    inside_key = (key_spots >= 0) & (key_spots < grid_total)
    nearby = jnp.abs(query_spots[:, None] - key_spots[None, :]) <= window
    return (
        nearby
        & (query_seg[:, None] == key_seg[None, :])
        & inside_query[:, None]
        & inside_key[None, :]
    )


def both_sides(query_head, key_head, value_head, grad_head, allowed):
    factor = query_head.shape[1] ** (-0.5)
    scores = inner_last(query_head, key_head) * factor
    scores = jnp.where(allowed, scores, NEG_FILL)
    row_peak = jnp.max(scores, axis=1, keepdims=True)
    exp_scores = jnp.exp(scores - row_peak)
    attn_probs = exp_scores / jnp.sum(exp_scores, axis=1, keepdims=True)
    probs_low = attn_probs.astype(jnp.bfloat16)
    attended = jnp.dot(probs_low, value_head, preferred_element_type=jnp.float32).astype(
        jnp.bfloat16
    )
    row_drift = jnp.sum(
        grad_head.astype(jnp.float32) * attended.astype(jnp.float32), axis=1, keepdims=True
    )
    value_grad = inner_first(probs_low, grad_head)
    prob_grad = inner_last(grad_head, value_head)
    score_grad = (attn_probs * (prob_grad - row_drift)).astype(jnp.bfloat16)
    query_grad = jnp.dot(score_grad, key_head, preferred_element_type=jnp.float32) * factor
    key_grad = inner_first(score_grad, query_head) * factor
    return (query_grad, key_grad, value_grad, attended)


def split_heads(block):
    rows_count = block.shape[0]
    return block.reshape(rows_count, HEADS, -1).transpose(1, 0, 2)


def join_heads(block):
    head_count, rows_count, head_width = block.shape
    return block.transpose(1, 0, 2).reshape(rows_count, head_count * head_width)


def body(queries, keys, values, out_grad, proj_weight, lengths):
    frames = queries.shape[1]
    shards = lax.axis_size("seq")
    grid_total = frames * shards
    own_index = lax.axis_index("seq")
    window = WINDOW
    grad_rows = out_grad[0]
    grad_attn = jnp.dot(grad_rows, proj_weight, preferred_element_type=jnp.float32).astype(
        jnp.bfloat16
    )
    utter_ends = jnp.cumsum(lengths[0])
    own_spots = own_index * frames + jnp.arange(frames, dtype=jnp.int32)
    wide_spots = own_index * frames - window + jnp.arange(frames + 2 * window, dtype=jnp.int32)
    allowed = visible(own_spots, wide_spots, utter_ends, grid_total, window)
    stacked = jnp.stack([keys, values])
    padded = extended(stacked, (("seq", 2),), window)

    def per_head(slices):
        return both_sides(slices[0], slices[1], slices[2], slices[3], allowed)

    query_grad, key_grad, value_grad, attended = lax.map(
        per_head,
        (
            split_heads(queries[0]),
            split_heads(padded[0, 0]),
            split_heads(padded[1, 0]),
            split_heads(grad_attn),
        ),
    )
    grad_sums = jnp.stack([join_heads(key_grad), join_heads(value_grad)])
    from_below = from_behind(grad_sums[:, frames + window :].astype(jnp.bfloat16), "seq", 1).astype(
        jnp.float32
    )
    from_above = from_behind(grad_sums[:, :window].astype(jnp.bfloat16), "seq", -1).astype(
        jnp.float32
    )
    middle = grad_sums[:, window : window + frames]
    middle = middle + jnp.pad(from_below, ((0, 0), (0, frames - window), (0, 0)))
    middle = middle + jnp.pad(from_above, ((0, 0), (frames - window, 0), (0, 0)))
    attended_rows = join_heads(attended)
    weight_grad = lax.psum_scatter(
        inner_first(grad_rows, attended_rows), ("seq", "dp"), scatter_dimension=0, tiled=True
    )
    query_out = join_heads(query_grad).astype(jnp.bfloat16)[None]
    key_out = middle[0].astype(jnp.bfloat16)[None]
    value_out = middle[1].astype(jnp.bfloat16)[None]
    return (query_out, key_out, value_out, weight_grad)


def solution(mesh):
    in_specs = (
        P("dp", "seq", None),
        P("dp", "seq", None),
        P("dp", "seq", None),
        P("dp", "seq", None),
        P(),
        P("dp", None),
    )
    out_specs = (
        P("dp", "seq", None),
        P("dp", "seq", None),
        P("dp", "seq", None),
        P(("seq", "dp"), None),
    )
    return jax.shard_map(body, mesh=mesh, in_specs=in_specs, out_specs=out_specs, check_vma=False)
```

profile of v0, /device:TPU:0, one launch (start us, length us, event | category | flops | bytes accessed | tf_op | source)
XLA Modules:
  0.0 336.5 jit_solution(14706541751062091677)
XLA Ops:
  8.9 2.4 copy.42
  11.2 2.7 fusion.43
  13.9 5.8 %collective-permute-start = (bf16[2,1,256,1024]{2,3,1,0:T(8,128)(2,1)}, bf16[2,1,256,1024]{2,3,1,0:T(8,128)(2,1)}, u32[]{:S(2)}, u32[]{:S(2)}) collective-permute-start(bf16[2,1,256,1024]{2,3,1,0:T(8,128)(2,1)} %get-tuple-element.202), channel_id=1, source_target_pairs={{0,2},{2,4},{4,6},{6,8},{8,10},{10,12},{12,14},{14,16},{16,18},{18... | collective-permute-start | bytes 3145736 | tf_op jit(solution)/shard_map/ppermute | solution.py:20
  21.4 2.3 copy.40
  23.7 3.1 convolution_convert_fusion.1
  26.7 2.4 copy.52
  29.3 34.6 %collective-permute-done = bf16[2,1,256,1024]{2,3,1,0:T(8,128)(2,1)} collective-permute-done((bf16[2,1,256,1024]{2,3,1,0:T(8,128)(2,1)}, bf16[2,1,256,1024]{2,3,1,0:T(8,128)(2,1)}, u32[]{:S(2)}, u32[]{:S(2)}) %collective-permute-start) | collective-permute-done | bytes 1048608 | tf_op jit(solution)/shard_map/ppermute | solution.py:20
  67.6 2.2 fusion.48
  69.8 93.2 %while.17 = (s32[]{:T(128)}, bf16[8,384,128]{2,1,0:T(8,128)(2,1)}, f32[8,896,128]{2,1,0:T(8,128)}, f32[8,896,128]{2,1,0:T(8,128)}, bf16[8,384,128]{1,2,0:T(8,128...) while((s32[]{:T(128)}, bf16[8,384,128]{2,1,0:T(8,128)(2,1)}, ...), condition=%wide.region_7.8_spmd.clone, body=%wide.region_3.7_spmd.clone.sunk | while | flops 536804224 | bytes 11798433 | solution.py:114
  77.1 2.3 fusion.81
  88.8 2.3 fusion.81
  100.4 2.3 fusion.81
  112.1 2.3 fusion.81
  114.4 2.1 fusion.80
  123.8 2.3 fusion.81
  126.0 2.1 fusion.80
  135.4 2.3 fusion.81
  147.1 2.3 fusion.81
  158.7 2.3 fusion.81
  161.0 2.1 fusion.80
  163.1 4.4 %convolution_bitcast_fusion.1 = f32[1024,1024]{0,1:T(8,128)} fusion(bf16[384,1024]{0,1:T(8,128)(2,1)S(1)} %bitcast.121, bf16[1,384,1024]{2,1,0:T(8,128)(2,1)} %param.11), kind=kOutput, calls=%fused_computation.52 | convolution fusion | flops 805306368 | bytes 5767168 | tf_op jit(solution)/shard_map/dot_general | solution.py:39
  167.5 5.3 %copy.53 = f32[1024,1024]{1,0:T(8,128)} copy(f32[1024,1024]{0,1:T(8,128)} %convolution_bitcast_fusion.1) | data formatting | bytes 8388608
  172.8 6.0 %copy.49 = f32[896,8,128]{2,1,0:T(8,128)} copy(f32[896,8,128]{2,0,1:T(8,128)} %bitcast.118) | data formatting | bytes 7340032 | tf_op jit(solution)/shard_map/transpose | solution.py:91
  178.9 4.8 %stack_reshape.6 = f32[1,896,1024]{2,1,0:T(8,128)} reshape(f32[896,8,128]{2,1,0:T(8,128)} %copy.49) | data formatting | bytes 7340032 | tf_op jit(solution)/shard_map/stack;reshape | solution.py:123
  183.7 6.0 %copy.50 = f32[896,8,128]{2,1,0:T(8,128)} copy(f32[896,8,128]{2,0,1:T(8,128)} %bitcast.117) | data formatting | bytes 7340032 | tf_op jit(solution)/shard_map/transpose | solution.py:91
  189.7 4.7 %stack_reshape.7 = f32[1,896,1024]{2,1,0:T(8,128)} reshape(f32[896,8,128]{2,1,0:T(8,128)} %copy.50) | data formatting | bytes 7340032 | tf_op jit(solution)/shard_map/stack;reshape | solution.py:123
  194.4 2.7 constant_dynamic-update-slice_fusion.1
  198.7 2.4 copy-done.2
  202.3 3.4 %collective-permute-start.2 = (bf16[2,256,1024]{2,1,0:T(8,128)(2,1)}, bf16[2,256,1024]{2,1,0:T(8,128)(2,1)S(1)}, u32[]{:S(2)}, u32[]{:S(2)}) collective-permute-start(bf16[2,256,1024]{2,1,0:T(8,128)(2,1)} %get-tuple-element.196), channel_id=1, source_target_pairs={{0,2},{2,4},{4,6},{6,8},{8,10},{10,12},{12,14},{14,16},{16,18},{18... | collective-permute-start | bytes 3145736 | tf_op jit(solution)/shard_map/ppermute | solution.py:29
  208.8 56.9 %collective-permute-done.2 = bf16[2,256,1024]{2,1,0:T(8,128)(2,1)S(1)} collective-permute-done((bf16[2,256,1024]{2,1,0:T(8,128)(2,1)}, bf16[2,256,1024]{2,1,0:T(8,128)(2,1)S(1)}, u32[]{:S(2)}, u32[]{:S(2)}) %collective-permute-start.2) | collective-permute-done | bytes 1048608 | tf_op jit(solution)/shard_map/ppermute | solution.py:29
  265.7 2.9 fusion.42
  269.9 59.7 %reduce-scatter.4.cloned.1.call-done = f32[32,1024]{1,0:T(8,128)} async-done(((f32[1024,1024]{1,0:T(8,128)}), f32[32,1024]{1,0:T(8,128)}) %reduce-scatter.4.cloned.1.call-update) | async-done | bytes 131088
  (95 shorter events, 82.8 us)
Async XLA Ops:
  7.2 16.5 %copy-start = (bf16[1024,1024]{1,0:T(8,128)(2,1)S(1)}, bf16[1024,1024]{1,0:T(8,128)(2,1)}, u32[]{:S(2)}) copy-start(bf16[1024,1024]{1,0:T(8,128)(2,1)} %param.12) | copy-start | bytes 6291460
  7.2 322.4 %reduce-scatter.4.cloned.1.call-start = ((), (), s32[]{:S(2)}) async-start(), calls=%async_computation.1 | async-start | bytes 4325376
  11.2 9.9 %copy-start.7 = (s32[1,32]{1,0:T(1,128)S(1)}, s32[1,32]{1,0:T(1,128)}, u32[]{:S(2)}) copy-start(s32[1,32]{1,0:T(1,128)} %param.13) | copy-start | bytes 388
  13.9 50.0 %collective-permute-start = (bf16[2,1,256,1024]{2,3,1,0:T(8,128)(2,1)}, bf16[2,1,256,1024]{2,3,1,0:T(8,128)(2,1)}, u32[]{:S(2)}, u32[]{:S(2)}) collective-permute-start(bf16[2,1,256,1024]{2,3,1,0:T(8,128)(2,1)} %get-tuple-element.202), channel_id=1, source_target_pairs={{0,2},{2,4},{4,6},{6,8},{8,10},{10,12},{12,14},{14,16},{16,18},{18... | collective-permute-start | bytes 3145736 | tf_op jit(solution)/shard_map/ppermute | solution.py:20
  19.8 46.1 %collective-permute-start.1 = (bf16[2,1,256,1024]{2,3,1,0:T(8,128)(2,1)}, bf16[2,1,256,1024]{2,3,1,0:T(8,128)(2,1)}, u32[]{:S(2)}, u32[]{:S(2)}) collective-permute-start(bf16[2,1,256,1024]{2,3,1,0:T(8,128)(2,1)} %get-tuple-element.203), channel_id=1, source_target_pairs={{2,0},{4,2},{6,4},{8,6},{10,8},{12,10},{14,12},{16,14},{18,16},{20... | collective-permute-start | bytes 3145736 | tf_op jit(solution)/shard_map/ppermute | solution.py:21
  26.7 39.2 %copy-start.4 = (bf16[1,384,1024]{1,2,0:T(8,128)(2,1)S(1)}, bf16[1,384,1024]{1,2,0:T(8,128)(2,1)}, u32[]{:S(2)}) copy-start(bf16[1,384,1024]{1,2,0:T(8,128)(2,1)} %copy.42) | copy-start | bytes 2359300
  67.6 2.2 copy-start.5
  194.4 3.2 copy-start.3
  198.1 3.0 copy-start.2
  201.1 6.0 %copy-start.6 = (bf16[8,384,128]{2,1,0:T(8,128)(2,1)S(1)}, bf16[8,384,128]{2,1,0:T(8,128)(2,1)}, u32[]{:S(2)}) copy-start(bf16[8,384,128]{2,1,0:T(8,128)(2,1)} %get-tuple-element.59) | copy-start | bytes 2359300
  202.3 63.4 %collective-permute-start.2 = (bf16[2,256,1024]{2,1,0:T(8,128)(2,1)}, bf16[2,256,1024]{2,1,0:T(8,128)(2,1)S(1)}, u32[]{:S(2)}, u32[]{:S(2)}) collective-permute-start(bf16[2,256,1024]{2,1,0:T(8,128)(2,1)} %get-tuple-element.196), channel_id=1, source_target_pairs={{0,2},{2,4},{4,6},{6,8},{8,10},{10,12},{12,14},{14,16},{16,18},{18... | collective-permute-start | bytes 3145736 | tf_op jit(solution)/shard_map/ppermute | solution.py:29
  205.7 59.9 %collective-permute-start.3 = (bf16[2,256,1024]{2,1,0:T(8,128)(2,1)S(1)}, bf16[2,256,1024]{2,1,0:T(8,128)(2,1)}, u32[]{:S(2)}, u32[]{:S(2)}) collective-permute-start(bf16[2,256,1024]{2,1,0:T(8,128)(2,1)S(1)} %get-tuple-element.197), channel_id=1, source_target_pairs={{2,0},{4,2},{6,4},{8,6},{10,8},{12,10},{14,12},{16,14},{18,16},{20... | collective-permute-start | bytes 3145736 | tf_op jit(solution)/shard_map/ppermute | solution.py:29
  265.7 64.0 %copy-start.1 = (bf16[1024,1024]{1,0:T(8,128)(2,1)S(1)}, bf16[1024,1024]{1,0:T(8,128)(2,1)}, u32[]{:S(2)}) copy-start(bf16[1024,1024]{1,0:T(8,128)(2,1)} %param.12) | copy-start | bytes 6291460
Sparse Core Ops, SparseCore 0:
  173.0 156.6 reduce-scatter.3
where the time goes:
time: 338 us; the launch traced here: 336 us
  waiting for transfers between devices  153 us (45%)
  matrix products  97.2 us (29%)
  local copies, waits for them, and re-layouts  48.3 us (14%)
  between operations  14.2 us (4%)
  starting transfers between devices  11.9 us (4%)
  other arithmetic  11.5 us (3%)
    unnamed x2, waiting for transfers between devices  59.7 us
    ppermute x2, waiting for transfers between devices, from_behind(): return lax.ppermute(shard, axis, pairs)  56.9 us
    dot_general x17, matrix products, inner_first(): lax.dot_general(left, right, (((0,), (0,)), ((), ())), preferred_element_...  39.1 us
    ppermute x1, waiting for transfers between devices, extended(): before = lax.ppermute(last, axis, up)  34.6 us
    dot_general x16, matrix products, inner_last(): lax.dot_general(left, right, (((1,), (1,)), ((), ())), preferred_element_...  26.8 us
    unnamed x21, local copies, waits for them, and re-layouts  17.2 us
    dot_general x8, matrix products, both_sides(): jnp.dot(score_grad, key_head, preferred_element_type=jnp.float32) * factor  15.7 us
    dot_general x8, matrix products, both_sides(): jnp.dot(probs_low, value_head, preferred_element_type=jnp.float32)  12.6 us
  transfers between devices with their start and end apart: 5, of which 4 were waited for; matrix products, arithmetic and copies ran while one was open for 12% of the time, Pallas kernels for 0%

commit v1 on v0

v1 whole, which is shorter than its diff:
```python
import functools

import jax
import jax.numpy as jnp
from jax import lax
from jax.experimental import pallas as pl
from jax.experimental.pallas import tpu as pltpu
from jax.sharding import PartitionSpec as P

HEADS = 8
WINDOW = 256
GROUP = 2
NEG_FILL = -1e30
MESH = pl.DeviceIdType.MESH


def dot(left, right, left_dim, right_dim):
    return lax.dot_general(
        left, right, (((left_dim,), (right_dim,)), ((), ())), preferred_element_type=jnp.float32
    )


def iota(shape, dim):
    return lax.broadcasted_iota(jnp.int32, shape, dim)


def fill_bias(bias, lengths_ref, me, frames):
    utts = lengths_ref.shape[1]
    lens = lengths_ref[...].astype(jnp.float32)
    upto = iota((utts, utts), 1) <= iota((utts, utts), 0)
    ends_col = jnp.sum(jnp.where(upto, lens, 0.0), axis=1, keepdims=True)
    same = iota((utts, utts), 1) == iota((utts, utts), 0)
    ends_row = jnp.sum(jnp.where(same, ends_col, 0.0), axis=0, keepdims=True)
    wide = bias.shape[1]
    last = ends_row[:, utts - 1 :]
    first = me * frames
    query_spots = first + iota((frames, 1), 0)
    key_spots = first - WINDOW + iota((1, wide), 1)
    query_at = query_spots.astype(jnp.float32)
    key_at = key_spots.astype(jnp.float32)
    query_seg = jnp.sum(jnp.where(ends_row <= query_at, 1.0, 0.0), axis=1, keepdims=True)
    key_seg = jnp.sum(jnp.where(ends_col <= key_at, 1.0, 0.0), axis=0, keepdims=True)
    key_seg = jnp.where((key_at >= 0.0) & (key_at < last), key_seg, -1.0)
    step = 128
    for r in range(0, frames, step):
        near = jnp.abs(query_at[r : r + step] - key_at) <= float(WINDOW)
        seen = near & (query_seg[r : r + step] == key_seg)
        bias[r : r + step, :] = jnp.where(seen, 0.0, NEG_FILL)


def kernel(
    n, inside,
    q_ref, k_ref, v_ref, g_ref, w_ref, lengths_ref,
    dq_ref, dk_ref, dv_ref, wg_ref,
    bias, ga, gt, att, key_acc, value_acc,
    halo_l, halo_r, out_l, out_r, ret_l, ret_r,
    halo_send, halo_recv, ret_send, ret_recv,
    *scatter,
):
    me = lax.axis_index("seq")
    core = lax.axis_index("dp")
    frames, width = q_ref.shape
    head = width // HEADS
    cols = GROUP * head
    groups = HEADS // GROUP
    factor = head ** (-0.5)
    has_l = me > 0
    has_r = me < n - 1
    left = jnp.maximum(me - 1, 0)
    right = jnp.minimum(me + 1, n - 1)
    if inside:
        x, y = lax.rem(me, 2), lax.rem(me // 2, 2)
        z0, z1 = lax.rem(me // 4, 2), me // 8
        partners = (
            (me, 1 - core),
            (me + 2 - 4 * y, core),
            (me + 4 - 8 * z0, core),
            (me + 8 - 16 * z1, core),
            (me + 1 - 2 * x, core),
        )
    else:
        partners = ()

    barrier = pltpu.get_barrier_semaphore()

    @pl.when(has_l)
    def _():
        pl.semaphore_signal(barrier, inc=1, device_id=(left, core), device_id_type=MESH)

    @pl.when(has_r)
    def _():
        pl.semaphore_signal(barrier, inc=1, device_id=(right, core), device_id_type=MESH)

    for partner in partners:
        pl.semaphore_signal(barrier, inc=1, device_id=partner, device_id_type=MESH)
    greeted = jnp.where(has_l, 1, 0) + jnp.where(has_r, 1, 0) + len(partners)
    pl.semaphore_wait(barrier, greeted)

    def halo_copy(which, side, g):
        src = (k_ref, v_ref)[which]
        rows = pl.ds(0, WINDOW) if side == 0 else pl.ds(frames - WINDOW, WINDOW)
        return pltpu.make_async_remote_copy(
            src_ref=src.at[rows, pl.ds(pl.multiple_of(g * cols, cols), cols)],
            dst_ref=(halo_r, halo_l)[side].at[which, g],
            send_sem=halo_send.at[which, side, g],
            recv_sem=halo_recv.at[which, side, g],
            device_id=((left, right)[side], core),
            device_id_type=MESH,
        )

    def ret_copy(which, side, g):
        return pltpu.make_async_remote_copy(
            src_ref=(out_l, out_r)[side].at[which, g],
            dst_ref=(ret_r, ret_l)[side].at[which, g],
            send_sem=ret_send.at[which, side, g],
            recv_sem=ret_recv.at[which, side, g],
            device_id=((left, right)[side], core),
            device_id_type=MESH,
        )

    def start_halos(g, _):
        @pl.when(has_l)
        def _():
            halo_copy(0, 0, g).start()
            halo_copy(1, 0, g).start()

        @pl.when(has_r)
        def _():
            halo_copy(0, 1, g).start()
            halo_copy(1, 1, g).start()

        return 0

    lax.fori_loop(0, groups, start_halos, 0)

    @pl.when(jnp.logical_not(has_l))
    def _():
        halo_l[...] = jnp.zeros_like(halo_l)
        ret_l[...] = jnp.zeros_like(ret_l)

    @pl.when(jnp.logical_not(has_r))
    def _():
        halo_r[...] = jnp.zeros_like(halo_r)
        ret_r[...] = jnp.zeros_like(ret_r)

    fill_bias(bias, lengths_ref, me, frames)
    gt[...] = g_ref[...].T

    def project(g, _):
        at = pl.ds(pl.multiple_of(g * cols, cols), cols)
        ga[:, at] = dot(g_ref[...], w_ref[:, at], 1, 0).astype(jnp.bfloat16)
        return 0

    lax.fori_loop(0, groups, project, 0)

    def one_group(g, _):
        @pl.when(has_l)
        def _():
            halo_copy(0, 1, g).wait_recv()
            halo_copy(1, 1, g).wait_recv()

        @pl.when(has_r)
        def _():
            halo_copy(0, 0, g).wait_recv()
            halo_copy(1, 0, g).wait_recv()

        for part in range(GROUP):
            at = pl.ds(pl.multiple_of(g * cols + part * head, head), head)
            inner = slice(part * head, (part + 1) * head)
            q = q_ref[:, at]
            grad = ga[:, at]
            key = jnp.concatenate([halo_l[0, g, :, inner], k_ref[:, at], halo_r[0, g, :, inner]], axis=0)
            value = jnp.concatenate([halo_l[1, g, :, inner], v_ref[:, at], halo_r[1, g, :, inner]], axis=0)
            scores = dot(q, key, 1, 1) * factor + bias[...]
            peak = jnp.max(scores, axis=1, keepdims=True)
            raised = jnp.exp(scores - peak)
            probs = raised * (1.0 / jnp.sum(raised, axis=1, keepdims=True))
            low = probs.astype(jnp.bfloat16)
            attended = dot(low, value, 1, 0).astype(jnp.bfloat16)
            att[:, at] = attended
            drift = jnp.sum(
                grad.astype(jnp.float32) * attended.astype(jnp.float32), axis=1, keepdims=True
            )
            value_grad = dot(low, grad, 0, 0)
            score_grad = (probs * (dot(grad, value, 1, 1) - drift)).astype(jnp.bfloat16)
            dq_ref[:, at] = (dot(score_grad, key, 1, 0) * factor).astype(jnp.bfloat16)
            key_grad = dot(score_grad, q, 0, 0) * factor
            for which, total, acc in ((0, key_grad, key_acc), (1, value_grad, value_acc)):
                out_l[which, g, :, inner] = total[:WINDOW].astype(jnp.bfloat16)
                acc[:, at] = total[WINDOW : WINDOW + frames]
                out_r[which, g, :, inner] = total[WINDOW + frames :].astype(jnp.bfloat16)

        @pl.when(has_l)
        def _():
            ret_copy(0, 0, g).start()
            ret_copy(1, 0, g).start()

        @pl.when(has_r)
        def _():
            ret_copy(0, 1, g).start()
            ret_copy(1, 1, g).start()

        return 0

    lax.fori_loop(0, groups, one_group, 0)

    if inside:
        wg, sums, send0, recv0, send1, recv1, send2, recv2, send3, recv3, send4, recv4, sc_send, sc_recv = scatter
        sends = (send0, send1, send2, send3, send4)
        recvs = (recv0, recv1, recv2, recv3, recv4)
    else:
        wg = wg_ref

    def weight(g, _):
        at = pl.ds(pl.multiple_of(g * cols, cols), cols)
        wg[:, at] = dot(gt[...], att[:, at], 1, 0)
        return 0

    lax.fori_loop(0, groups, weight, 0)

    if inside:
        block = wg_ref.shape[0]

        def exchange(step):
            return pltpu.make_async_remote_copy(
                src_ref=sends[step],
                dst_ref=recvs[step],
                send_sem=sc_send.at[step],
                recv_sem=sc_recv.at[step],
                device_id=partners[step],
                device_id_type=MESH,
            )

        def rows_of(s, c):
            return pl.ds(pl.multiple_of((s * 2 + c) * block, block), block)

        def pack0(s, _):
            send0[s] = wg[rows_of(s, 1 - core), :].astype(jnp.bfloat16)
            return 0

        lax.fori_loop(0, n, pack0, 0)
        exchange(0).start()
        exchange(0).wait_recv()

        def add0(s, _):
            sums[s] = wg[rows_of(s, core), :] + recv0[s].astype(jnp.float32)
            return 0

        lax.fori_loop(0, n, add0, 0)

        spots = (
            (8, lambda i, b: (i // 2) * 4 + b * 2 + lax.rem(i, 2), y),
            (4, lambda i, b: (i // 2) * 8 + b * 4 + y * 2 + lax.rem(i, 2), z0),
            (2, lambda i, b: b * 8 + z0 * 4 + y * 2 + i, z1),
            (1, lambda i, b: z1 * 8 + z0 * 4 + y * 2 + b + i * 0, x),
        )
        for t, (count, spot, bit) in enumerate(spots, 1):
            def pack(i, _):
                sends[t][i] = sums[spot(i, 1 - bit)].astype(jnp.bfloat16)
                return 0

            lax.fori_loop(0, count, pack, 0)
            exchange(t).start()
            exchange(t).wait_recv()

            def add(i, _):
                at = spot(i, bit)
                sums[at] = sums[at] + recvs[t][i].astype(jnp.float32)
                return 0

            lax.fori_loop(0, count, add, 0)
        wg_ref[...] = sums[me]
        for t in range(len(partners)):
            exchange(t).wait_send()

    def finish(g, _):
        @pl.when(has_l)
        def _():
            for which in range(2):
                ret_copy(which, 1, g).wait_recv()
                ret_copy(which, 0, g).wait_send()
                halo_copy(which, 0, g).wait_send()

        @pl.when(has_r)
        def _():
            for which in range(2):
                ret_copy(which, 0, g).wait_recv()
                ret_copy(which, 1, g).wait_send()
                halo_copy(which, 1, g).wait_send()

        at = pl.ds(pl.multiple_of(g * cols, cols), cols)
        for which, acc, out in ((0, key_acc, dk_ref), (1, value_acc, dv_ref)):
            total = acc[:, at]
            pad = jnp.zeros((frames - WINDOW, cols), jnp.float32)
            total = total + jnp.concatenate([ret_l[which, g].astype(jnp.float32), pad], axis=0)
            total = total + jnp.concatenate([pad, ret_r[which, g].astype(jnp.float32)], axis=0)
            out[:, at] = total.astype(jnp.bfloat16)
        return 0

    lax.fori_loop(0, groups, finish, 0)


def body(n, dp, queries, keys, values, out_grad, proj_weight, lengths):
    frames, width = queries.shape[1:]
    head = width // HEADS
    cols = GROUP * head
    groups = HEADS // GROUP
    inside = n == 16 and dp == 2
    block = width // (n * dp)
    wide = frames + 2 * WINDOW
    bf16, f32 = jnp.bfloat16, jnp.float32
    halo = pltpu.VMEM((2, groups, WINDOW, cols), bf16)
    sems = pltpu.SemaphoreType.DMA((2, 2, groups))
    scratch = [
        pltpu.VMEM((frames, wide), f32),
        pltpu.VMEM((frames, width), bf16),
        pltpu.VMEM((width, frames), bf16),
        pltpu.VMEM((frames, width), bf16),
        pltpu.VMEM((frames, width), f32),
        pltpu.VMEM((frames, width), f32),
        halo, halo, halo, halo, halo, halo,
        sems, sems, sems, sems,
    ]
    if inside:
        scratch += [pltpu.VMEM((width, width), f32), pltpu.VMEM((n, block, width), f32)]
        for count in (16, 8, 4, 2, 1):
            scratch += [pltpu.VMEM((count, block, width), bf16)] * 2
        scratch += [pltpu.SemaphoreType.DMA((5,))] * 2
    wg_shape = (block, width) if inside else (width, width)
    vmem = pl.BlockSpec(memory_space=pltpu.VMEM)
    dq, dk, dv, wg = pl.pallas_call(
        functools.partial(kernel, n, inside),
        out_shape=[jax.ShapeDtypeStruct((frames, width), bf16)] * 3
        + [jax.ShapeDtypeStruct(wg_shape, f32)],
        in_specs=[vmem] * 6,
        out_specs=[vmem] * 4,
        scratch_shapes=scratch,
        compiler_params=pltpu.CompilerParams(
            collective_id=0, has_side_effects=True, vmem_limit_bytes=56 * 1024 * 1024
        ),
    )(queries[0], keys[0], values[0], out_grad[0], proj_weight, lengths)
    if not inside:
        wg = lax.psum_scatter(wg, ("seq", "dp"), scatter_dimension=0, tiled=True)
    return dq[None], dk[None], dv[None], wg


def solution(mesh):
    rows = P("dp", "seq", None)
    return jax.shard_map(
        functools.partial(body, mesh.shape["seq"], mesh.shape["dp"]),
        mesh=mesh,
        in_specs=(rows, rows, rows, rows, P(), P("dp", None)),
        out_specs=(rows, rows, rows, P(("seq", "dp"), None)),
        check_vma=False,
    )
```

time: 338 us -> 123 us (0.36)
  waiting for transfers between devices: 153 us -> 0 us
  Pallas kernels: 0 us -> 118 us
  matrix products: 97.2 us -> 0 us
  local copies, waits for them, and re-layouts: 48.3 us -> 4.61 us
  between operations: 14.2 us -> 0.67 us
  starting transfers between devices: 11.9 us -> 0 us
  other arithmetic: 11.5 us -> 0 us
    pallas_call x0 -> x1, Pallas kernels: none -> 118 us  [body(): pl.pallas_call(functools.partial(kernel, n, inside), out_shape=[jax.Shape...]
    dot_general x50 -> x0, matrix products: 97.2 us -> none  [the longest x17 39.1 us: inner_first(): lax.dot_general(left, right, (((0,), (0,)), ((), ())), preferred_element_...]
    ppermute x4 -> x0, waiting for transfers between devices: 93.5 us -> none  [the longest x2 56.9 us: from_behind(): return lax.ppermute(shard, axis, pairs)]
    unnamed x2 -> x0, waiting for transfers between devices: 59.7 us -> none
    unnamed x21 -> x10, local copies, waits for them, and re-layouts: 17.2 us -> 4.61 us
    transpose x2 -> x0, local copies, waits for them, and re-layouts: 12.1 us -> none  [join_heads(): return block.transpose(1, 0, 2).reshape(rows_count, head_count * head_width)]
    ppermute x4 -> x0, starting transfers between devices: 11.9 us -> none  [the longest x1 5.85 us: extended(): before = lax.ppermute(last, axis, up)]
    another operation x4 -> x0, local copies, waits for them, and re-layouts: 10 us -> none  [the longest x3 9.95 us: body(): grad_sums = jnp.stack([join_heads(key_grad), join_heads(value_grad)])]
  transfers between devices with their start and end apart: 5 -> 0, of which waited for: 4 -> 0; matrix products, arithmetic and copies ran while one was open for 12% -> 0% of each run, Pallas kernels for 0% -> 0%
where the time goes in v1:
time: 123 us
  Pallas kernels  118 us (96%)
  local copies, waits for them, and re-layouts  4.61 us (4%)
    pallas_call x1, Pallas kernels, body(): pl.pallas_call(functools.partial(kernel, n, inside), out_shape=[jax.Shape...  118 us
    unnamed x10, local copies, waits for them, and re-layouts  4.61 us

profile of v1, /device:TPU:0, one launch (start us, length us, event | category | flops | bytes accessed | tf_op | source)
XLA Modules:
  0.0 122.9 jit_solution(18307391379685716842)
XLA Ops:
  0.6 117.6 %shard_map.93 = (bf16[384,1024]{1,0:T(8,128)(2,1)}, bf16[384,1024]{1,0:T(8,128)(2,1)}, bf16[384,1024]{1,0:T(8,128)(2,1)}, f32[32,1024]{1,0:T(8,128)}) custom-call(bf16[384,1024]{1,0:T(8,128)(2,1)} %bitcast.10, bf16[384,1024]{1,0:T(8,128)(2,1)} %bitcast.11, bf16[384,1024]{1,0:T(8,128)(2,1)} %bitcast.12, bf16[384,1024]{1,0:T(8,128)(2,1)} %bitcast.13, ...), custom_call_target="tpu_custom_call" | custom-call | tf_op jit(solution)/shard_map/pallas_call | solution.py:331
  118.2 0.0 copy-start.1
  118.2 0.0 copy-start
  118.2 0.0 copy-start.2
  118.3 2.2 %copy.14 = bf16[1,384,1024]{2,1,0:T(8,128)(2,1)} copy(bf16[1,384,1024]{2,1,0:T(8,128)(2,1)} %bitcast.9) | data formatting | bytes 1572864
  120.4 0.0 copy-done.1
  120.4 0.9 copy.15
  121.3 0.0 copy-done
  121.3 0.9 copy.16
  122.2 0.0 copy-done.2
  122.2 0.7 copy.17
Async XLA Ops:
  118.2 2.2 %copy-start.1 = (bf16[384,1024]{1,0:T(8,128)(2,1)S(1)}, bf16[384,1024]{1,0:T(8,128)(2,1)}, u32[]{:S(2)}) copy-start(bf16[384,1024]{1,0:T(8,128)(2,1)} %get-tuple-element.9) | copy-start | bytes 2359300
  118.2 3.1 %copy-start = (bf16[384,1024]{1,0:T(8,128)(2,1)S(1)}, bf16[384,1024]{1,0:T(8,128)(2,1)}, u32[]{:S(2)}) copy-start(bf16[384,1024]{1,0:T(8,128)(2,1)} %get-tuple-element.10) | copy-start | bytes 2359300
  118.2 4.0 %copy-start.2 = (f32[32,1024]{1,0:T(8,128)S(1)}, f32[32,1024]{1,0:T(8,128)}, u32[]{:S(2)}) copy-start(f32[32,1024]{1,0:T(8,128)} %get-tuple-element.19) | copy-start | bytes 393220

commit v2 on v1

--- a/solution.py
+++ b/solution.py
@@ -52,9 +52,11 @@
     n, inside,
     q_ref, k_ref, v_ref, g_ref, w_ref, lengths_ref,
     dq_ref, dk_ref, dv_ref, wg_ref,
-    bias, ga, gt, att, key_acc, value_acc,
-    halo_l, halo_r, out_l, out_r, ret_l, ret_r,
-    halo_send, halo_recv, ret_send, ret_recv,
+    bias, ga, gt, att, query_acc,
+    grad_l, grad_r, halo_l, halo_r, out_l, out_r, ret_l, ret_r,
+    local, final, part_l, part_r, got_l, got_r, done_l, done_r, told_l, told_r,
+    grad_send, grad_recv, halo_send, halo_recv, ret_send, ret_recv,
+    part_send, part_recv, done_send, done_recv,
     *scatter,
 ):
     me = lax.axis_index("seq")
@@ -68,6 +70,7 @@
     has_r = me < n - 1
     left = jnp.maximum(me - 1, 0)
     right = jnp.minimum(me + 1, n - 1)
+    low_end, high_end = WINDOW, WINDOW + frames
     if inside:
         x, y = lax.rem(me, 2), lax.rem(me // 2, 2)
         z0, z1 = lax.rem(me // 4, 2), me // 8
@@ -96,113 +99,196 @@
     greeted = jnp.where(has_l, 1, 0) + jnp.where(has_r, 1, 0) + len(partners)
     pl.semaphore_wait(barrier, greeted)
 
-    def halo_copy(which, side, g):
-        src = (k_ref, v_ref)[which]
-        rows = pl.ds(0, WINDOW) if side == 0 else pl.ds(frames - WINDOW, WINDOW)
+    edges = (pl.ds(0, WINDOW), pl.ds(frames - WINDOW, WINDOW))
+
+    def copy(side, src, dst, send, recv):
         return pltpu.make_async_remote_copy(
-            src_ref=src.at[rows, pl.ds(pl.multiple_of(g * cols, cols), cols)],
-            dst_ref=(halo_r, halo_l)[side].at[which, g],
-            send_sem=halo_send.at[which, side, g],
-            recv_sem=halo_recv.at[which, side, g],
+            src_ref=src,
+            dst_ref=dst,
+            send_sem=send,
+            recv_sem=recv,
             device_id=((left, right)[side], core),
             device_id_type=MESH,
         )
 
-    def ret_copy(which, side, g):
-        return pltpu.make_async_remote_copy(
-            src_ref=(out_l, out_r)[side].at[which, g],
-            dst_ref=(ret_r, ret_l)[side].at[which, g],
-            send_sem=ret_send.at[which, side, g],
-            recv_sem=ret_recv.at[which, side, g],
-            device_id=((left, right)[side], core),
-            device_id_type=MESH,
-        )
+    def grad_copy(side, _):
+        return copy(side, g_ref.at[edges[side], :], (grad_r, grad_l)[side],
+                    grad_send.at[side], grad_recv.at[side])
+
+    def halo_copy(side, g):
+        at = pl.ds(pl.multiple_of(g * cols, cols), cols)
+        return copy(side, q_ref.at[edges[side], at], (halo_r, halo_l)[side].at[g],
+                    halo_send.at[side, g], halo_recv.at[side, g])
+
+    def part_copy(side, b):
+        return copy(side, (part_l, part_r)[side].at[b], (got_r, got_l)[side].at[b],
+                    part_send.at[side, b], part_recv.at[side, b])
+
+    def done_copy(side, b):
+        return copy(side, (done_l, done_r)[side].at[b], (told_r, told_l)[side].at[b],
+                    done_send.at[side, b], done_recv.at[side, b])
+
+    def ret_copy(side, g):
+        return copy(side, (out_l, out_r)[side].at[g], (ret_r, ret_l)[side].at[g],
+                    ret_send.at[side, g], ret_recv.at[side, g])
+
+    def start(make, i):
+        @pl.when(has_l)
+        def _():
+            make(0, i).start()
+
+        @pl.when(has_r)
+        def _():
+            make(1, i).start()
+
+    def arrive(make, i):
+        @pl.when(has_l)
+        def _():
+            make(1, i).wait_recv()
+
+        @pl.when(has_r)
+        def _():
+            make(0, i).wait_recv()
+
+    def sent(make, i):
+        @pl.when(has_l)
+        def _():
+            make(0, i).wait_send()
+
+        @pl.when(has_r)
+        def _():
+            make(1, i).wait_send()
+
+    start(grad_copy, 0)
 
     def start_halos(g, _):
-        @pl.when(has_l)
-        def _():
-            halo_copy(0, 0, g).start()
-            halo_copy(1, 0, g).start()
-
-        @pl.when(has_r)
-        def _():
-            halo_copy(0, 1, g).start()
-            halo_copy(1, 1, g).start()
-
+        start(halo_copy, g)
         return 0
 
     lax.fori_loop(0, groups, start_halos, 0)
+
+    blank = jnp.where(iota((2, 16, WINDOW), 1) < 4, NEG_FILL, 0.0)
 
     @pl.when(jnp.logical_not(has_l))
     def _():
-        halo_l[...] = jnp.zeros_like(halo_l)
-        ret_l[...] = jnp.zeros_like(ret_l)
+        for ref in (grad_l, halo_l, ret_l, told_l):
+            ref[...] = jnp.zeros_like(ref)
+        got_l[...] = blank
 
     @pl.when(jnp.logical_not(has_r))
     def _():
-        halo_r[...] = jnp.zeros_like(halo_r)
-        ret_r[...] = jnp.zeros_like(ret_r)
+        for ref in (grad_r, halo_r, ret_r, told_r):
+            ref[...] = jnp.zeros_like(ref)
+        got_r[...] = blank
 
     fill_bias(bias, lengths_ref, me, frames)
-    gt[...] = g_ref[...].T
-
-    def project(g, _):
-        at = pl.ds(pl.multiple_of(g * cols, cols), cols)
-        ga[:, at] = dot(g_ref[...], w_ref[:, at], 1, 0).astype(jnp.bfloat16)
+    part_l[...] = jnp.zeros_like(part_l)
+    part_r[...] = jnp.zeros_like(part_r)
+
+    def project(ref, first, rows):
+        gt[:, first : first + rows] = ref[...].T
+
+        def some(g, _):
+            at = pl.ds(pl.multiple_of(g * cols, cols), cols)
+            ga[first : first + rows, at] = dot(ref[...], w_ref[:, at], 1, 0).astype(jnp.bfloat16)
+            return 0
+
+        lax.fori_loop(0, groups, some, 0)
+
+    project(g_ref, low_end, frames)
+    arrive(grad_copy, 0)
+    project(grad_l, 0, WINDOW)
+    project(grad_r, high_end, WINDOW)
+
+    def operands(g, part):
+        at = pl.ds(pl.multiple_of(g * cols + part * head, head), head)
+        inner = slice(part * head, (part + 1) * head)
+        query = jnp.concatenate([halo_l[g, :, inner], q_ref[:, at], halo_r[g, :, inner]], axis=0)
+        return at, inner, query, ga[:, at], k_ref[:, at], v_ref[:, at]
+
+    def first_pass(g, _):
+        arrive(halo_copy, g)
+        for part in range(GROUP):
+            at, inner, query, grad, key, value = operands(g, part)
+            scores = dot(key, query, 1, 1) * factor + bias[...]
+            peak = jnp.max(scores, axis=0, keepdims=True)
+            raised = jnp.exp(scores - peak)
+            h = g * GROUP + part
+            local[h, 0:1, :] = peak
+            local[h, 1:2, :] = jnp.sum(raised, axis=0, keepdims=True)
+            local[h, 2:3, :] = jnp.sum(raised * dot(value, grad, 1, 1), axis=0, keepdims=True)
         return 0
 
-    lax.fori_loop(0, groups, project, 0)
-
-    def one_group(g, _):
-        @pl.when(has_l)
-        def _():
-            halo_copy(0, 1, g).wait_recv()
-            halo_copy(1, 1, g).wait_recv()
-
-        @pl.when(has_r)
-        def _():
-            halo_copy(0, 0, g).wait_recv()
-            halo_copy(1, 0, g).wait_recv()
-
+    def send_parts(b):
+        for i in range(4):
+            for j in range(3):
+                row = local[b * 4 + i, j : j + 1, :]
+                part_l[b, j * 4 + i : j * 4 + i + 1, :] = row[:, :low_end]
+                part_r[b, j * 4 + i : j * 4 + i + 1, :] = row[:, high_end:]
+        start(part_copy, b)
+
+    def merge(b):
+        arrive(part_copy, b)
+        for i in range(4):
+            def three(j, empty):
+                pad = jnp.full((1, frames - WINDOW), empty, jnp.float32)
+                at = slice(j * 4 + i, j * 4 + i + 1)
+                return (
+                    local[b * 4 + i, j : j + 1, low_end:high_end],
+                    jnp.concatenate([got_l[b, at, :], pad], axis=1),
+                    jnp.concatenate([pad, got_r[b, at, :]], axis=1),
+                )
+
+            peaks = three(0, NEG_FILL)
+            peak = jnp.maximum(jnp.maximum(peaks[0], peaks[1]), peaks[2])
+            scales = [jnp.exp(p - peak) for p in peaks]
+            total = sum(a * c for a, c in zip(scales, three(1, 0.0)))
+            drift = sum(a * c for a, c in zip(scales, three(2, 0.0))) / total
+            level = peak + jnp.log(total)
+            for j, row in ((0, level), (1, drift)):
+                final[b * 4 + i, j : j + 1, low_end:high_end] = row
+                done_l[b, j * 4 + i : j * 4 + i + 1, :] = row[:, :WINDOW]
+                done_r[b, j * 4 + i : j * 4 + i + 1, :] = row[:, frames - WINDOW :]
+        start(done_copy, b)
+
+    def unpack(b):
+        arrive(done_copy, b)
+        for i in range(4):
+            for j in range(2):
+                at = slice(j * 4 + i, j * 4 + i + 1)
+                final[b * 4 + i, j : j + 1, :low_end] = told_l[b, at, :]
+                final[b * 4 + i, j : j + 1, high_end:] = told_r[b, at, :]
+
+    def second_pass(g, _):
         for part in range(GROUP):
-            at = pl.ds(pl.multiple_of(g * cols + part * head, head), head)
-            inner = slice(part * head, (part + 1) * head)
-            q = q_ref[:, at]
-            grad = ga[:, at]
-            key = jnp.concatenate([halo_l[0, g, :, inner], k_ref[:, at], halo_r[0, g, :, inner]], axis=0)
-            value = jnp.concatenate([halo_l[1, g, :, inner], v_ref[:, at], halo_r[1, g, :, inner]], axis=0)
-            scores = dot(q, key, 1, 1) * factor + bias[...]
-            peak = jnp.max(scores, axis=1, keepdims=True)
-            raised = jnp.exp(scores - peak)
-            probs = raised * (1.0 / jnp.sum(raised, axis=1, keepdims=True))
+            at, inner, query, grad, key, value = operands(g, part)
+            h = g * GROUP + part
+            scores = dot(key, query, 1, 1) * factor + bias[...]
+            probs = jnp.exp(scores - final[h, 0:1, :])
             low = probs.astype(jnp.bfloat16)
-            attended = dot(low, value, 1, 0).astype(jnp.bfloat16)
-            att[:, at] = attended
-            drift = jnp.sum(
-                grad.astype(jnp.float32) * attended.astype(jnp.float32), axis=1, keepdims=True
-            )
-            value_grad = dot(low, grad, 0, 0)
-            score_grad = (probs * (dot(grad, value, 1, 1) - drift)).astype(jnp.bfloat16)
-            dq_ref[:, at] = (dot(score_grad, key, 1, 0) * factor).astype(jnp.bfloat16)
-            key_grad = dot(score_grad, q, 0, 0) * factor
-            for which, total, acc in ((0, key_grad, key_acc), (1, value_grad, value_acc)):
-                out_l[which, g, :, inner] = total[:WINDOW].astype(jnp.bfloat16)
-                acc[:, at] = total[WINDOW : WINDOW + frames]
-                out_r[which, g, :, inner] = total[WINDOW + frames :].astype(jnp.bfloat16)
-
-        @pl.when(has_l)
-        def _():
-            ret_copy(0, 0, g).start()
-            ret_copy(1, 0, g).start()
-
-        @pl.when(has_r)
-        def _():
-            ret_copy(0, 1, g).start()
-            ret_copy(1, 1, g).start()
-
+            dv_ref[:, at] = dot(low, grad, 1, 0).astype(jnp.bfloat16)
+            att[:, at] = dot(low, value, 0, 0).astype(jnp.bfloat16)
+            score_grad = (probs * (dot(value, grad, 1, 1) - final[h, 1:2, :])).astype(jnp.bfloat16)
+            dk_ref[:, at] = (dot(score_grad, query, 1, 0) * factor).astype(jnp.bfloat16)
+            total = dot(score_grad, key, 0, 0) * factor
+            out_l[g, :, inner] = total[:low_end].astype(jnp.bfloat16)
+            query_acc[:, at] = total[low_end:high_end]
+            out_r[g, :, inner] = total[high_end:].astype(jnp.bfloat16)
+        start(ret_copy, g)
         return 0
 
-    lax.fori_loop(0, groups, one_group, 0)
+    lax.fori_loop(0, 2, first_pass, 0)
+    send_parts(0)
+    lax.fori_loop(2, 3, first_pass, 0)
+    merge(0)
+    lax.fori_loop(3, 4, first_pass, 0)
+    send_parts(1)
+    unpack(0)
+    lax.fori_loop(0, 1, second_pass, 0)
+    merge(1)
+    lax.fori_loop(1, 2, second_pass, 0)
+    unpack(1)
+    lax.fori_loop(2, 4, second_pass, 0)
 
     if inside:
         wg, sums, send0, recv0, send1, recv1, send2, recv2, send3, recv3, send4, recv4, sc_send, sc_recv = scatter
@@ -274,30 +360,22 @@
             exchange(t).wait_send()
 
     def finish(g, _):
-        @pl.when(has_l)
-        def _():
-            for which in range(2):
-                ret_copy(which, 1, g).wait_recv()
-                ret_copy(which, 0, g).wait_send()
-                halo_copy(which, 0, g).wait_send()
-
-        @pl.when(has_r)
-        def _():
-            for which in range(2):
-                ret_copy(which, 0, g).wait_recv()
-                ret_copy(which, 1, g).wait_send()
-                halo_copy(which, 1, g).wait_send()
-
+        arrive(ret_copy, g)
+        sent(ret_copy, g)
+        sent(halo_copy, g)
         at = pl.ds(pl.multiple_of(g * cols, cols), cols)
-        for which, acc, out in ((0, key_acc, dk_ref), (1, value_acc, dv_ref)):
-            total = acc[:, at]
-            pad = jnp.zeros((frames - WINDOW, cols), jnp.float32)
-            total = total + jnp.concatenate([ret_l[which, g].astype(jnp.float32), pad], axis=0)
-            total = total + jnp.concatenate([pad, ret_r[which, g].astype(jnp.float32)], axis=0)
-            out[:, at] = total.astype(jnp.bfloat16)
+        pad = jnp.zeros((frames - WINDOW, cols), jnp.float32)
+        total = query_acc[:, at]
+        total = total + jnp.concatenate([ret_l[g].astype(jnp.float32), pad], axis=0)
+        total = total + jnp.concatenate([pad, ret_r[g].astype(jnp.float32)], axis=0)
+        dq_ref[:, at] = total.astype(jnp.bfloat16)
         return 0
 
     lax.fori_loop(0, groups, finish, 0)
+    sent(grad_copy, 0)
+    for b in range(2):
+        sent(part_copy, b)
+        sent(done_copy, b)
 
 
 def body(n, dp, queries, keys, values, out_grad, proj_weight, lengths):
@@ -309,17 +387,22 @@
     block = width // (n * dp)
     wide = frames + 2 * WINDOW
     bf16, f32 = jnp.bfloat16, jnp.float32
-    halo = pltpu.VMEM((2, groups, WINDOW, cols), bf16)
-    sems = pltpu.SemaphoreType.DMA((2, 2, groups))
+    edge = pltpu.VMEM((WINDOW, width), bf16)
+    halo = pltpu.VMEM((groups, WINDOW, cols), bf16)
+    stat = pltpu.VMEM((HEADS, 8, wide), f32)
+    parts = pltpu.VMEM((2, 16, WINDOW), f32)
+    done = pltpu.VMEM((2, 8, WINDOW), f32)
+    one, some = pltpu.SemaphoreType.DMA((2,)), pltpu.SemaphoreType.DMA((2, groups))
+    two = pltpu.SemaphoreType.DMA((2, 2))
     scratch = [
         pltpu.VMEM((frames, wide), f32),
-        pltpu.VMEM((frames, width), bf16),
-        pltpu.VMEM((width, frames), bf16),
-        pltpu.VMEM((frames, width), bf16),
+        pltpu.VMEM((wide, width), bf16),
+        pltpu.VMEM((width, wide), bf16),
+        pltpu.VMEM((wide, width), bf16),
         pltpu.VMEM((frames, width), f32),
-        pltpu.VMEM((frames, width), f32),
-        halo, halo, halo, halo, halo, halo,
-        sems, sems, sems, sems,
+        edge, edge, halo, halo, halo, halo, halo, halo,
+        stat, stat, parts, parts, parts, parts, done, done, done, done,
+        one, one, some, some, some, some, two, two, two, two,
     ]
     if inside:
         scratch += [pltpu.VMEM((width, width), f32), pltpu.VMEM((n, block, width), f32)]

time: 123 us -> 119 us (0.967)
  Pallas kernels: 118 us -> 114 us
    pallas_call x1, Pallas kernels: 118 us -> 114 us  [body(): pl.pallas_call(functools.partial(kernel, n, inside), out_shape=[jax.Shape...]
where the time goes in v2:
time: 119 us
  Pallas kernels  114 us (96%)
  local copies, waits for them, and re-layouts  4.61 us (4%)
    pallas_call x1, Pallas kernels, body(): pl.pallas_call(functools.partial(kernel, n, inside), out_shape=[jax.Shape...  114 us
    unnamed x10, local copies, waits for them, and re-layouts  4.61 us

profile of v2, /device:TPU:0, one launch (start us, length us, event | category | flops | bytes accessed | tf_op | source)
XLA Modules:
  0.0 118.8 jit_solution(12067817784524704722)
XLA Ops:
  0.6 113.5 %shard_map.93 = (bf16[384,1024]{1,0:T(8,128)(2,1)}, bf16[384,1024]{1,0:T(8,128)(2,1)}, bf16[384,1024]{1,0:T(8,128)(2,1)}, f32[32,1024]{1,0:T(8,128)}) custom-call(bf16[384,1024]{1,0:T(8,128)(2,1)} %bitcast.10, bf16[384,1024]{1,0:T(8,128)(2,1)} %bitcast.11, bf16[384,1024]{1,0:T(8,128)(2,1)} %bitcast.12, bf16[384,1024]{1,0:T(8,128)(2,1)} %bitcast.13, ...), custom_call_target="tpu_custom_call" | custom-call | tf_op jit(solution)/shard_map/pallas_call | solution.py:414
  114.2 0.0 copy-start.1
  114.2 0.0 copy-start
  114.2 0.0 copy-start.2
  114.2 2.2 %copy.14 = bf16[1,384,1024]{2,1,0:T(8,128)(2,1)} copy(bf16[1,384,1024]{2,1,0:T(8,128)(2,1)} %bitcast.9) | data formatting | bytes 1572864
  116.4 0.0 copy-done.1
  116.4 0.9 copy.15
  117.2 0.0 copy-done
  117.3 0.9 copy.16
  118.1 0.0 copy-done.2
  118.1 0.7 copy.17
Async XLA Ops:
  114.2 2.2 %copy-start.1 = (bf16[384,1024]{1,0:T(8,128)(2,1)S(1)}, bf16[384,1024]{1,0:T(8,128)(2,1)}, u32[]{:S(2)}) copy-start(bf16[384,1024]{1,0:T(8,128)(2,1)} %get-tuple-element.9) | copy-start | bytes 2359300
  114.2 3.1 %copy-start = (bf16[384,1024]{1,0:T(8,128)(2,1)S(1)}, bf16[384,1024]{1,0:T(8,128)(2,1)}, u32[]{:S(2)}) copy-start(bf16[384,1024]{1,0:T(8,128)(2,1)} %get-tuple-element.10) | copy-start | bytes 2359300
  114.2 4.0 %copy-start.2 = (f32[32,1024]{1,0:T(8,128)S(1)}, f32[32,1024]{1,0:T(8,128)}, u32[]{:S(2)}) copy-start(f32[32,1024]{1,0:T(8,128)} %get-tuple-element.19) | copy-start | bytes 393220

commit v3 on v2

--- a/solution.py
+++ b/solution.py
@@ -277,6 +277,78 @@
         start(ret_copy, g)
         return 0
 
+    if inside:
+        wg, sums, send0, recv0, send1, recv1, send2, recv2, send3, recv3, send4, recv4, sc_send, sc_recv = scatter
+        sends = (send0, send1, send2, send3, send4)
+        recvs = (recv0, recv1, recv2, recv3, recv4)
+    else:
+        wg = wg_ref
+    block = wg_ref.shape[0]
+    half = width // 2
+
+    def weight(b):
+        def some(g, _):
+            at = pl.ds(pl.multiple_of(g * cols, cols), cols)
+            wg[:, at] = dot(gt[...], att[:, at], 1, 0)
+            return 0
+
+        lax.fori_loop(b * 2, b * 2 + 2, some, 0)
+
+    def exchange(t, b):
+        return pltpu.make_async_remote_copy(
+            src_ref=sends[t].at[b],
+            dst_ref=recvs[t].at[b],
+            send_sem=sc_send.at[t, b],
+            recv_sem=sc_recv.at[t, b],
+            device_id=partners[t],
+            device_id_type=MESH,
+        )
+
+    def rows_of(s, c):
+        return pl.ds(pl.multiple_of((s * 2 + c) * block, block), block)
+
+    if inside:
+        spots = (
+            (n, None, None),
+            (8, lambda i, b: (i // 2) * 4 + b * 2 + lax.rem(i, 2), y),
+            (4, lambda i, b: (i // 2) * 8 + b * 4 + y * 2 + lax.rem(i, 2), z0),
+            (2, lambda i, b: b * 8 + z0 * 4 + y * 2 + i, z1),
+            (1, lambda i, b: z1 * 8 + z0 * 4 + y * 2 + b + i * 0, x),
+        )
+
+    def begin(t, b):
+        if not inside:
+            return
+        count, spot, bit = spots[t]
+        at = slice(b * half, (b + 1) * half)
+
+        def pack(i, _):
+            if t == 0:
+                sends[0][b, i] = wg[rows_of(i, 1 - core), at].astype(jnp.bfloat16)
+            else:
+                sends[t][b, i] = sums[spot(i, 1 - bit), :, at].astype(jnp.bfloat16)
+            return 0
+
+        lax.fori_loop(0, count, pack, 0)
+        exchange(t, b).start()
+
+    def end(t, b):
+        if not inside:
+            return
+        count, spot, bit = spots[t]
+        at = slice(b * half, (b + 1) * half)
+        exchange(t, b).wait_recv()
+
+        def add(i, _):
+            if t == 0:
+                sums[i, :, at] = wg[rows_of(i, core), at] + recvs[0][b, i].astype(jnp.float32)
+            else:
+                to = spot(i, bit)
+                sums[to, :, at] = sums[to, :, at] + recvs[t][b, i].astype(jnp.float32)
+            return 0
+
+        lax.fori_loop(0, count, add, 0)
+
     lax.fori_loop(0, 2, first_pass, 0)
     send_parts(0)
     lax.fori_loop(2, 3, first_pass, 0)
@@ -287,77 +359,36 @@
     lax.fori_loop(0, 1, second_pass, 0)
     merge(1)
     lax.fori_loop(1, 2, second_pass, 0)
+    weight(0)
+    begin(0, 0)
     unpack(1)
-    lax.fori_loop(2, 4, second_pass, 0)
-
+    lax.fori_loop(2, 3, second_pass, 0)
+    end(0, 0)
+    begin(1, 0)
+    lax.fori_loop(3, 4, second_pass, 0)
+    weight(1)
+    begin(0, 1)
+    end(1, 0)
+    begin(2, 0)
+    end(0, 1)
+    begin(1, 1)
+    end(2, 0)
+    begin(3, 0)
+    end(3, 0)
+    begin(4, 0)
+    end(1, 1)
+    begin(2, 1)
+    end(4, 0)
+    end(2, 1)
+    begin(3, 1)
+    end(3, 1)
+    begin(4, 1)
+    end(4, 1)
     if inside:
-        wg, sums, send0, recv0, send1, recv1, send2, recv2, send3, recv3, send4, recv4, sc_send, sc_recv = scatter
-        sends = (send0, send1, send2, send3, send4)
-        recvs = (recv0, recv1, recv2, recv3, recv4)
-    else:
-        wg = wg_ref
-
-    def weight(g, _):
-        at = pl.ds(pl.multiple_of(g * cols, cols), cols)
-        wg[:, at] = dot(gt[...], att[:, at], 1, 0)
-        return 0
-
-    lax.fori_loop(0, groups, weight, 0)
-
-    if inside:
-        block = wg_ref.shape[0]
-
-        def exchange(step):
-            return pltpu.make_async_remote_copy(
-                src_ref=sends[step],
-                dst_ref=recvs[step],
-                send_sem=sc_send.at[step],
-                recv_sem=sc_recv.at[step],
-                device_id=partners[step],
-                device_id_type=MESH,
-            )
-
-        def rows_of(s, c):
-            return pl.ds(pl.multiple_of((s * 2 + c) * block, block), block)
-
-        def pack0(s, _):
-            send0[s] = wg[rows_of(s, 1 - core), :].astype(jnp.bfloat16)
-            return 0
-
-        lax.fori_loop(0, n, pack0, 0)
-        exchange(0).start()
-        exchange(0).wait_recv()
-
-        def add0(s, _):
-            sums[s] = wg[rows_of(s, core), :] + recv0[s].astype(jnp.float32)
-            return 0
-
-        lax.fori_loop(0, n, add0, 0)
-
-        spots = (
-            (8, lambda i, b: (i // 2) * 4 + b * 2 + lax.rem(i, 2), y),
-            (4, lambda i, b: (i // 2) * 8 + b * 4 + y * 2 + lax.rem(i, 2), z0),
-            (2, lambda i, b: b * 8 + z0 * 4 + y * 2 + i, z1),
-            (1, lambda i, b: z1 * 8 + z0 * 4 + y * 2 + b + i * 0, x),
-        )
-        for t, (count, spot, bit) in enumerate(spots, 1):
-            def pack(i, _):
-                sends[t][i] = sums[spot(i, 1 - bit)].astype(jnp.bfloat16)
-                return 0
-
-            lax.fori_loop(0, count, pack, 0)
-            exchange(t).start()
-            exchange(t).wait_recv()
-
-            def add(i, _):
-                at = spot(i, bit)
-                sums[at] = sums[at] + recvs[t][i].astype(jnp.float32)
-                return 0
-
-            lax.fori_loop(0, count, add, 0)
         wg_ref[...] = sums[me]
         for t in range(len(partners)):
-            exchange(t).wait_send()
+            exchange(t, 0).wait_send()
+            exchange(t, 1).wait_send()
 
     def finish(g, _):
         arrive(ret_copy, g)
@@ -407,8 +438,8 @@
     if inside:
         scratch += [pltpu.VMEM((width, width), f32), pltpu.VMEM((n, block, width), f32)]
         for count in (16, 8, 4, 2, 1):
-            scratch += [pltpu.VMEM((count, block, width), bf16)] * 2
-        scratch += [pltpu.SemaphoreType.DMA((5,))] * 2
+            scratch += [pltpu.VMEM((2, count, block, width // 2), bf16)] * 2
+        scratch += [pltpu.SemaphoreType.DMA((5, 2))] * 2
     wg_shape = (block, width) if inside else (width, width)
     vmem = pl.BlockSpec(memory_space=pltpu.VMEM)
     dq, dk, dv, wg = pl.pallas_call(

time: 119 us -> 111 us (0.933)
  Pallas kernels: 114 us -> 106 us
    pallas_call x1, Pallas kernels: 114 us -> 106 us  [body(): pl.pallas_call(functools.partial(kernel, n, inside), out_shape=[jax.Shape...]
where the time goes in v3:
time: 111 us
  Pallas kernels  106 us (95%)
  local copies, waits for them, and re-layouts  4.61 us (4%)
    pallas_call x1, Pallas kernels, body(): pl.pallas_call(functools.partial(kernel, n, inside), out_shape=[jax.Shape...  106 us
    unnamed x10, local copies, waits for them, and re-layouts  4.61 us

profile of v3, /device:TPU:0, one launch (start us, length us, event | category | flops | bytes accessed | tf_op | source)
XLA Modules:
  0.0 110.8 jit_solution(8752142563289833601)
XLA Ops:
  0.6 105.5 %shard_map.93 = (bf16[384,1024]{1,0:T(8,128)(2,1)}, bf16[384,1024]{1,0:T(8,128)(2,1)}, bf16[384,1024]{1,0:T(8,128)(2,1)}, f32[32,1024]{1,0:T(8,128)}) custom-call(bf16[384,1024]{1,0:T(8,128)(2,1)} %bitcast.10, bf16[384,1024]{1,0:T(8,128)(2,1)} %bitcast.11, bf16[384,1024]{1,0:T(8,128)(2,1)} %bitcast.12, bf16[384,1024]{1,0:T(8,128)(2,1)} %bitcast.13, ...), custom_call_target="tpu_custom_call" | custom-call | tf_op jit(solution)/shard_map/pallas_call | solution.py:445
  106.2 0.0 copy-start.1
  106.2 0.0 copy-start
  106.2 0.0 copy-start.2
  106.2 2.2 %copy.14 = bf16[1,384,1024]{2,1,0:T(8,128)(2,1)} copy(bf16[1,384,1024]{2,1,0:T(8,128)(2,1)} %bitcast.9) | data formatting | bytes 1572864
  108.4 0.0 copy-done.1
  108.4 0.9 copy.15
  109.3 0.0 copy-done
  109.3 0.9 copy.16
  110.1 0.0 copy-done.2
  110.1 0.7 copy.17
Async XLA Ops:
  106.2 2.2 %copy-start.1 = (bf16[384,1024]{1,0:T(8,128)(2,1)S(1)}, bf16[384,1024]{1,0:T(8,128)(2,1)}, u32[]{:S(2)}) copy-start(bf16[384,1024]{1,0:T(8,128)(2,1)} %get-tuple-element.9) | copy-start | bytes 2359300
  106.2 3.1 %copy-start = (bf16[384,1024]{1,0:T(8,128)(2,1)S(1)}, bf16[384,1024]{1,0:T(8,128)(2,1)}, u32[]{:S(2)}) copy-start(bf16[384,1024]{1,0:T(8,128)(2,1)} %get-tuple-element.10) | copy-start | bytes 2359300
  106.2 4.0 %copy-start.2 = (f32[32,1024]{1,0:T(8,128)S(1)}, f32[32,1024]{1,0:T(8,128)}, u32[]{:S(2)}) copy-start(f32[32,1024]{1,0:T(8,128)} %get-tuple-element.19) | copy-start | bytes 393220
